TPU v7x, 512 devices: a whole 4x4x16 slice. The times are simulated.
512 devices in a mesh: dp: 32 (over y, x, core), tm: 16 (over z).
Axes of the slice: x: 4, y: 4, z: 16, core: 2. Of those that a mesh axis runs over, the one named last changes fastest.
Arguments:
- phonemes: bfloat16 [32, 256, 1024], P('dp', 'tm'), may hold values from -6 to 6
- durations: int32 [32, 256], P('dp', 'tm'), may hold values from 1 to 32, 2048 in all within a row
- conv_weight: bfloat16 [9, 1024, 2048], P(None, None, 'tm'), may hold values from -0.0625 to 0.0625
- out_weight: bfloat16 [2048, 1024], P('tm', 'dp'), may hold values from -0.125 to 0.125
- norm_gain: float32 [1024], replicated, may hold values from 0.1 to 1.9
Outputs:
- decoded: bfloat16 [32, 2048, 1024], P('dp', 'tm')
Inputs may be any that keep to these rules, and one draw needn't show every extreme that they name: Each utterance's durations sum to 2048, and in each utterance some phoneme lasts exactly 32 frames.
All inputs are finite; a program needn't handle non-finite values. No bound on the sum of `durations` on one device may be relied on, other than what follows from the above.
Results may differ from a plain program's by a relative error of at most 0.015.
Values may be sent and summed in bfloat16 or wider, within the bound.
A program may use at most 64 MiB of HBM per device.

v0:
```python
import jax
import jax.numpy as jnp
from jax import lax
from jax.sharding import PartitionSpec as P

KER = 9
FR = 128


def on_device(phonemes, durations, conv_weight, out_weight, norm_gain):
    margin = KER // 2
    rows_all, lengths_all = (
        lax.all_gather(phonemes, "tm", axis=1, tiled=True),
        lax.all_gather(durations, "tm", axis=1, tiled=True),
    )
    rows_all = rows_all[0]
    phone_lengths = lengths_all[0]
    phone_ends = jnp.cumsum(phone_lengths).astype(jnp.int32)
    phone_starts = phone_ends - phone_lengths
    total_frames = FR * lax.axis_size("tm")
    first_own = lax.axis_index("tm") * FR
    positions = first_own + jnp.arange(FR, dtype=jnp.int32)
    inside = (positions[:, None] >= phone_starts[None, :]) & (
        positions[:, None] < phone_ends[None, :]
    )
    own_rows = jnp.dot(
        inside.astype(jnp.bfloat16), rows_all, preferred_element_type=jnp.float32
    ).astype(jnp.bfloat16)
    frames = lax.all_gather(own_rows, "tm", axis=0, tiled=True)
    padded = jnp.pad(frames, ((margin, margin), (0, 0)))
    pre_act = jnp.zeros((total_frames, conv_weight.shape[2]), jnp.float32)
    for offset in range(KER):
        pre_act = pre_act + jnp.dot(
            padded[offset : offset + total_frames],
            conv_weight[offset],
            preferred_element_type=jnp.float32,
        )
    hidden = jnp.maximum(pre_act, 0.0).astype(jnp.bfloat16)
    columns = lax.all_gather(out_weight, "dp", axis=1, tiled=True)
    reduced = lax.psum_scatter(
        jnp.dot(hidden, columns, preferred_element_type=jnp.float32).astype(jnp.bfloat16),
        "tm",
        scatter_dimension=0,
        tiled=True,
    ).astype(jnp.float32)
    summed = own_rows.astype(jnp.float32) + reduced
    average = jnp.mean(summed, axis=-1, keepdims=True)
    centered = summed - average
    spread = jnp.mean(centered * centered, axis=-1, keepdims=True)
    decoded = centered * lax.rsqrt(spread + 1e-05) * norm_gain
    return decoded.astype(jnp.bfloat16)[None]


def solution(mesh):
    placed = (P("dp", "tm", None), P("dp", "tm"), P(None, None, "tm"), P("tm", "dp"), P())
    return jax.shard_map(
        on_device, mesh=mesh, in_specs=placed, out_specs=P("dp", "tm", None), check_vma=False
    )
```

profile of v0, /device:TPU:2, one launch (start us, length us, event | category | flops | bytes accessed | tf_op | source)
XLA Modules:
  0.0 252.1 jit_solution(1046039252529930426)
XLA Ops:
  6.5 0.0 all-gather.2.cloned.1.call-start
  6.5 1.3 dynamic-slice
  8.5 0.8 bitcast_dynamic-update-slice_fusion
  9.2 26.7 %all-reduce.1 = s32[256]{0:T(256)S(1)} all-reduce(s32[256]{0:T(256)S(1)} %bitcast_dynamic-update-slice_fusion), channel_id=1, replica_groups=mesh['dp'=32,'tm'=16] {'tm'}, use_global_device_ids=true, to_apply=%add.1 | all-reduce | flops 256 | bytes 2048
  35.9 0.3 reduce-window.9
  36.2 0.1 slice.59
  36.3 0.1 slice_reduce_fusion
  36.5 0.1 fusion.91
  36.5 0.1 broadcast_add_fusion
  36.6 30.0 %all_gather.13 = bf16[1,256,1024]{2,1,0:T(8,128)(2,1)S(1)} all-gather(bf16[1,16,1024]{2,1,0:T(8,128)(2,1)} %param.5), channel_id=1, replica_groups=mesh['dp'=32,'tm'=16] {'tm'}, dimensions={1}, use_global_device_ids=true | all-gather | bytes 557056 | tf_op jit(solution)/shard_map/all_gather | solution.py:13
  66.6 1.0 convolution_convert_fusion.1
  67.6 0.0 all-gather.2.cloned.1.call-update
  67.6 0.0 reduce-scatter.2.cloned.1.call-start
  67.6 24.8 %all_gather.15 = bf16[128,1024]{0,1:T(8,128)(2,1)S(1)} all-gather(bf16[128,32]{0,1:T(8,128)(2,1)} %param.8), channel_id=1, replica_groups=mesh['dp'=32,'tm'=16] {'dp'}, dimensions={1}, use_global_device_ids=true | all-gather | bytes 270336 | tf_op jit(solution)/shard_map/all_gather | solution.py:39
  92.4 0.0 copy-start.2
  92.4 51.4 %all-gather.2.cloned.1.call-done = bf16[2048,1024]{1,0:T(8,128)(2,1)} async-done(((bf16[128,1024]{1,0:T(8,128)(2,1)}), bf16[2048,1024]{1,0:T(8,128)(2,1)}) %all-gather.2.cloned.1.call-update) | async-done | bytes 4194320 | tf_op jit(solution)/shard_map/all_gather | solution.py:29
  143.8 0.0 copy-start
  143.8 3.6 %fusion.12 = f32[2048,128]{1,0:T(8,128)S(1)} fusion(bf16[2048,1024]{1,0:T(8,128)(2,1)} %all-gather.2.cloned.1.call-done, bf16[9,1024,128]{2,1,0:T(8,128)(2,1)} %param.7), kind=kOutput, calls=%fused_computation.12 | convolution fusion | flops 536870912 | bytes 5505024 | tf_op jit(solution)/shard_map/dot_general | solution.py:33
  147.5 0.0 copy-done.2
  147.5 0.0 copy-done
  147.5 1.3 fusion.10
  148.8 1.3 fusion.6
  150.1 1.3 fusion.4
  151.3 1.3 fusion.2
  152.6 1.3 fusion.22
  154.0 1.3 fusion.25
  155.2 2.3 fusion.18
  157.6 6.8 %convolution_convert_fusion = bf16[2048,1024]{1,0:T(8,128)(2,1)} fusion(bf16[128,1024]{0,1:T(8,128)(2,1)S(1)} %all_gather.15, f32[2048,128]{1,0:T(8,128)S(1)} %fusion.18, bf16[2048,1024]{1,0:T(8,128)(2,1)} %all-gather.2.cloned.1.call-done, bf16[9,1024,128]{2,1,0:T(8,128)(2,1)} %param.7), kind=kOutput, calls=%fused_computation.16 | convolution fusion | flops 1076625408 | bytes 9961472 | tf_op jit(solution)/shard_map/dot_general | solution.py:41
  164.3 0.0 copy-start.1
  164.3 0.0 copy-start.3
  164.3 0.0 reduce-scatter.2.cloned.1.call-update
  164.3 76.8 %reduce-scatter.2.cloned.1.call-done = bf16[128,1024]{1,0:T(8,128)(2,1)} async-done(((bf16[2048,1024]{1,0:T(8,128)(2,1)}), bf16[128,1024]{1,0:T(8,128)(2,1)}) %reduce-scatter.2.cloned.1.call-update) | async-done | bytes 262160 | tf_op jit(solution)/shard_map/reduce_scatter | solution.py:40
  241.2 0.0 copy-done.1
  241.2 1.1 fusion.51
  242.3 1.2 multiply_reduce_fusion
  243.4 0.0 copy-done.3
  243.4 1.8 fusion.52
  (6 shorter events, 0.1 us)
Async XLA Ops:
  6.5 137.3 %all-gather.2.cloned.1.call-start = ((), (), s32[]{:S(2)}) async-start(), calls=%async_computation.1 | async-start | bytes 4456448 | tf_op jit(solution)/shard_map/all_gather | solution.py:29
  67.6 173.6 %reduce-scatter.2.cloned.1.call-start = ((), (), s32[]{:S(2)}) async-start(), calls=%async_computation.2 | async-start | bytes 4456448 | tf_op jit(solution)/shard_map/reduce_scatter | solution.py:40
  92.4 55.1 %copy-start.2 = (bf16[9,1024,128]{2,1,0:T(8,128)(2,1)S(1)}, bf16[9,1024,128]{2,1,0:T(8,128)(2,1)}, u32[]{:S(2)}) copy-start(bf16[9,1024,128]{2,1,0:T(8,128)(2,1)} %param.7) | copy-start | bytes 7077892
  143.8 3.7 %copy-start = (bf16[2048,1024]{1,0:T(8,128)(2,1)S(1)}, bf16[2048,1024]{1,0:T(8,128)(2,1)}, u32[]{:S(2)}) copy-start(bf16[2048,1024]{1,0:T(8,128)(2,1)} %all-gather.2.cloned.1.call-done) | copy-start | bytes 12582916
  164.3 76.8 %copy-start.1 = (bf16[128,1024]{1,0:T(8,128)(2,1)S(1)}, bf16[128,1024]{1,0:T(8,128)(2,1)}, u32[]{:S(2)}) copy-start(bf16[128,1024]{1,0:T(8,128)(2,1)} %convolution_convert_fusion.1) | copy-start | bytes 786436
  164.3 79.1 %copy-start.3 = (f32[1024]{0:T(1024)S(1)}, f32[1024]{0:T(1024)}, u32[]{:S(2)}) copy-start(f32[1024]{0:T(1024)} %param.9) | copy-start | bytes 12292
Sparse Core Ops, SparseCore 0:
  67.7 76.0 all-gather.1
  164.5 76.6 reduce-scatter.1
where the time goes:
time: 252 us
  waiting for transfers between devices  128 us (51%)
  blocking collectives  81.5 us (32%)
  matrix products  21.4 us (8%)
  between operations  14.1 us (6%)
  other arithmetic  4.56 us (2%)
    reduce_scatter x1, waiting for transfers between devices, on_device(): lax.psum_scatter(jnp.dot(hidden, columns, preferred_element_type=jnp.floa...  76.8 us
    all_gather x1, waiting for transfers between devices, on_device(): frames = lax.all_gather(own_rows, 'tm', axis=0, tiled=True)  51.4 us
    all_gather x1, blocking collectives, on_device(): lax.all_gather(phonemes, 'tm', axis=1, tiled=True)  30 us
    unnamed x1, blocking collectives  26.7 us
    all_gather x1, blocking collectives, on_device(): columns = lax.all_gather(out_weight, 'dp', axis=1, tiled=True)  24.8 us
    dot_general x8, matrix products, on_device(): jnp.dot(padded[offset:offset + total_frames], conv_weight[offset], prefer...  13.7 us
    dot_general x1, matrix products, on_device(): jnp.dot(hidden, columns, preferred_element_type=jnp.float32)  6.75 us
  transfers between devices with their start and end apart: 2, of which 2 were waited for; matrix products, arithmetic and copies ran while one was open for 0% of the time, Pallas kernels for 0%

commit v1 on v0

--- a/solution.py
+++ b/solution.py
@@ -8,6 +8,33 @@
 
 
 def on_device(phonemes, durations, conv_weight, out_weight, norm_gain):
+
+    def expand_the_cubes(axis_k, here_x, axis_tag):
+        formed, t_next, taken_in = (
+            lax.axis_size(axis_tag),
+            lax.axis_index(axis_tag),
+            here_x.shape[axis_k],
+        )
+        samples = tuple(((no, (no + 1) % formed) for no in range(formed)))
+        queue = tuple(((no, (no - 1) % formed) for no in range(formed)))
+        arr_next = jnp.zeros(
+            (*here_x.shape[:axis_k], formed * taken_in, *here_x.shape[axis_k + 1 :]), here_x.dtype
+        )
+        arr_next = lax.dynamic_update_slice_in_dim(arr_next, here_x, t_next * taken_in, axis=axis_k)
+        newest = m_next = here_x
+        x_next = formed // 2
+        for dev in range(1, x_next + 1):
+            newest = lax.ppermute(newest, axis_tag, samples)
+            arr_next = lax.dynamic_update_slice_in_dim(
+                arr_next, newest, (t_next - dev) % formed * taken_in, axis=axis_k
+            )
+            if dev < formed - x_next:
+                m_next = lax.ppermute(m_next, axis_tag, queue)
+                arr_next = lax.dynamic_update_slice_in_dim(
+                    arr_next, m_next, (t_next + dev) % formed * taken_in, axis=axis_k
+                )
+        return arr_next
+
     margin = KER // 2
     rows_all, lengths_all = (
         lax.all_gather(phonemes, "tm", axis=1, tiled=True),
@@ -26,7 +53,7 @@
     own_rows = jnp.dot(
         inside.astype(jnp.bfloat16), rows_all, preferred_element_type=jnp.float32
     ).astype(jnp.bfloat16)
-    frames = lax.all_gather(own_rows, "tm", axis=0, tiled=True)
+    frames = expand_the_cubes(0, own_rows, "tm")
     padded = jnp.pad(frames, ((margin, margin), (0, 0)))
     pre_act = jnp.zeros((total_frames, conv_weight.shape[2]), jnp.float32)
     for offset in range(KER):

time: 252 us -> 305 us (1.21)
  the two profiles are of different devices: /device:TPU:2 before, /device:TPU:6 now
where the time goes in v1:
time: 305 us; the launch traced here: 304 us
  waiting for transfers between devices  92.1 us (30%)
  blocking collectives  81.8 us (27%)
  starting transfers between devices  52.9 us (17%)
  matrix products  43.3 us (14%)
  local copies, waits for them, and re-layouts  15.7 us (5%)
  between operations  14.2 us (5%)
  other arithmetic  4.56 us (1%)
    reduce_scatter x1, waiting for transfers between devices, on_device(): lax.psum_scatter(jnp.dot(hidden, columns, preferred_element_type=jnp.floa...  75.6 us
    ppermute x7, starting transfers between devices, expand_the_cubes(): m_next = lax.ppermute(m_next, axis_tag, queue)  36.3 us
    dot_general x8, matrix products, on_device(): jnp.dot(padded[offset:offset + total_frames], conv_weight[offset], prefer...  33.7 us
    all_gather x1, blocking collectives, on_device(): lax.all_gather(phonemes, 'tm', axis=1, tiled=True)  30.3 us
    unnamed x1, blocking collectives  26.7 us
    all_gather x1, blocking collectives, on_device(): columns = lax.all_gather(out_weight, 'dp', axis=1, tiled=True)  24.8 us
    ppermute x8, starting transfers between devices, expand_the_cubes(): newest = lax.ppermute(newest, axis_tag, samples)  16.5 us
    ppermute x8, waiting for transfers between devices, expand_the_cubes(): newest = lax.ppermute(newest, axis_tag, samples)  12.4 us
  transfers between devices with their start and end apart: 16, of which 8 were waited for; matrix products, arithmetic and copies ran while one was open for 3% of the time, Pallas kernels for 0%

profile of v1, /device:TPU:6, one launch (start us, length us, event | category | flops | bytes accessed | tf_op | source)
XLA Modules:
  0.0 304.4 jit_solution(15041255984495190238)
XLA Ops:
  6.5 1.3 dynamic-slice
  8.5 0.8 bitcast_dynamic-update-slice_fusion
  9.2 26.7 %all-reduce.1 = s32[256]{0:T(256)S(1)} all-reduce(s32[256]{0:T(256)S(1)} %bitcast_dynamic-update-slice_fusion), channel_id=1, replica_groups=mesh['dp'=32,'tm'=16] {'tm'}, use_global_device_ids=true, to_apply=%add.1 | all-reduce | flops 256 | bytes 2048
  36.6 30.3 %all_gather.10 = bf16[1,256,1024]{2,1,0:T(8,128)(2,1)S(1)} all-gather(bf16[1,16,1024]{2,1,0:T(8,128)(2,1)} %param.5), channel_id=1, replica_groups=mesh['dp'=32,'tm'=16] {'tm'}, dimensions={1}, use_global_device_ids=true | all-gather | bytes 557056 | tf_op jit(solution)/shard_map/all_gather | solution.py:40
  67.0 2.5 broadcast_in_dim.4
  69.5 1.0 constant_dynamic-update-slice_fusion.15
  70.4 3.0 collective-permute-start
  73.4 4.0 %collective-permute-start.1 = (bf16[128,1024]{1,0:T(8,128)(2,1)S(1)}, bf16[128,1024]{1,0:T(8,128)(2,1)S(1)}, u32[]{:S(2)}, u32[]{:S(2)}) collective-permute-start(bf16[128,1024]{1,0:T(8,128)(2,1)S(1)} %get-tuple-element.6), channel_id=1, source_target_pairs={{0,15},{1,0},{2,1},{3,2},{4,3},{5,4},{6,5},{7,6},{8,7},{9,8},{10,9... | collective-permute-start | bytes 786440 | tf_op jit(solution)/shard_map/ppermute | solution.py:32
  77.5 2.4 collective-permute-done
  79.9 1.9 collective-permute-start.2
  81.8 5.1 %collective-permute-start.3 = (bf16[128,1024]{1,0:T(8,128)(2,1)S(1)}, bf16[128,1024]{1,0:T(8,128)(2,1)S(1)}, u32[]{:S(2)}, u32[]{:S(2)}) collective-permute-start(bf16[128,1024]{1,0:T(8,128)(2,1)S(1)} %collective-permute-done.1), channel_id=1, source_target_pairs={{0,15},{1,0},{2,1},{3,2},{4,3},{5,4},{6,5},{7,6},{8,7},{9,8},{10,9... | collective-permute-start | bytes 786440 | tf_op jit(solution)/shard_map/ppermute | solution.py:32
  87.0 2.4 collective-permute-done.2
  89.4 1.9 collective-permute-start.4
  91.3 5.1 %collective-permute-start.5 = (bf16[128,1024]{1,0:T(8,128)(2,1)S(1)}, bf16[128,1024]{1,0:T(8,128)(2,1)S(1)}, u32[]{:S(2)}, u32[]{:S(2)}) collective-permute-start(bf16[128,1024]{1,0:T(8,128)(2,1)S(1)} %collective-permute-done.3), channel_id=1, source_target_pairs={{0,15},{1,0},{2,1},{3,2},{4,3},{5,4},{6,5},{7,6},{8,7},{9,8},{10,9... | collective-permute-start | bytes 786440 | tf_op jit(solution)/shard_map/ppermute | solution.py:32
  96.4 2.4 collective-permute-done.4
  98.8 1.9 collective-permute-start.6
  100.7 24.8 %all_gather.11 = bf16[128,1024]{0,1:T(8,128)(2,1)S(1)} all-gather(bf16[128,32]{0,1:T(8,128)(2,1)S(1)} %copy-done.1), channel_id=1, replica_groups=mesh['dp'=32,'tm'=16] {'dp'}, dimensions={1}, use_global_device_ids=true | all-gather | bytes 270336 | tf_op jit(solution)/shard_map/all_gather | solution.py:66
  125.5 0.7 constant_dynamic-update-slice_fusion.14
  126.2 5.2 %collective-permute-start.7 = (bf16[128,1024]{1,0:T(8,128)(2,1)S(1)}, bf16[128,1024]{1,0:T(8,128)(2,1)S(1)}, u32[]{:S(2)}, u32[]{:S(2)}) collective-permute-start(bf16[128,1024]{1,0:T(8,128)(2,1)S(1)} %collective-permute-done.5), channel_id=1, source_target_pairs={{0,15},{1,0},{2,1},{3,2},{4,3},{5,4},{6,5},{7,6},{8,7},{9,8},{10,9... | collective-permute-start | bytes 786440 | tf_op jit(solution)/shard_map/ppermute | solution.py:32
  132.2 1.9 collective-permute-start.8
  135.6 2.2 collective-permute-done.7
  137.7 5.6 %collective-permute-start.9 = (bf16[128,1024]{1,0:T(8,128)(2,1)S(1)}, bf16[128,1024]{1,0:T(8,128)(2,1)S(1)}, u32[]{:S(2)}, u32[]{:S(2)}) collective-permute-start(bf16[128,1024]{1,0:T(8,128)(2,1)S(1)} %collective-permute-done.7), channel_id=1, source_target_pairs={{0,15},{1,0},{2,1},{3,2},{4,3},{5,4},{6,5},{7,6},{8,7},{9,8},{10,9... | collective-permute-start | bytes 786440 | tf_op jit(solution)/shard_map/ppermute | solution.py:32
  144.1 1.9 collective-permute-start.10
  147.4 1.4 collective-permute-done.9
  148.8 5.6 %collective-permute-start.11 = (bf16[128,1024]{1,0:T(8,128)(2,1)S(1)}, bf16[128,1024]{1,0:T(8,128)(2,1)S(1)}, u32[]{:S(2)}, u32[]{:S(2)}) collective-permute-start(bf16[128,1024]{1,0:T(8,128)(2,1)S(1)} %collective-permute-done.9), channel_id=1, source_target_pairs={{0,15},{1,0},{2,1},{3,2},{4,3},{5,4},{6,5},{7,6},{8,7},{9,8},{10,9... | collective-permute-start | bytes 786440 | tf_op jit(solution)/shard_map/ppermute | solution.py:32
  155.1 1.9 collective-permute-start.12
  157.1 0.7 constant_dynamic-update-slice_fusion.6
  157.8 0.7 constant_dynamic-update-slice_fusion.5
  159.0 5.6 %collective-permute-start.13 = (bf16[128,1024]{1,0:T(8,128)(2,1)S(1)}, bf16[128,1024]{1,0:T(8,128)(2,1)S(1)}, u32[]{:S(2)}, u32[]{:S(2)}) collective-permute-start(bf16[128,1024]{1,0:T(8,128)(2,1)S(1)} %collective-permute-done.11), channel_id=1, source_target_pairs={{0,15},{1,0},{2,1},{3,2},{4,3},{5,4},{6,5},{7,6},{8,7},{9,8},{10,9... | collective-permute-start | bytes 786440 | tf_op jit(solution)/shard_map/ppermute | solution.py:32
  164.6 0.7 constant_dynamic-update-slice_fusion.4
  165.4 2.1 collective-permute-start.14
  167.5 0.7 constant_dynamic-update-slice_fusion.3
  168.9 0.7 constant_dynamic-update-slice_fusion.1
  169.7 5.2 %collective-permute-done.14 = bf16[128,1024]{1,0:T(8,128)(2,1)S(1)} collective-permute-done((bf16[128,1024]{1,0:T(8,128)(2,1)S(1)}, bf16[128,1024]{1,0:T(8,128)(2,1)S(1)}, u32[]{:S(2)}, u32[]{:S(2)}) %collective-permute-start.14) | collective-permute-done | bytes 262176 | tf_op jit(solution)/shard_map/ppermute | solution.py:27
  174.8 0.7 constant_dynamic-update-slice_fusion
  175.6 3.5 %fusion.12 = f32[2048,128]{1,0:T(8,128)S(1)} fusion(bf16[2048,1024]{1,0:T(8,128)(2,1)} %constant_dynamic-update-slice_fusion, bf16[9,1024,128]{2,1,0:T(8,128)(2,1)S(1)} %copy-done), kind=kOutput, calls=%fused_computation.12 | convolution fusion | flops 536870912 | bytes 5505024 | tf_op jit(solution)/shard_map/dot_general | solution.py:60
  179.0 4.4 %fusion.10 = f32[2048,128]{1,0:T(8,128)} fusion(bf16[2048,1024]{1,0:T(8,128)(2,1)} %constant_dynamic-update-slice_fusion, bf16[9,1024,128]{2,1,0:T(8,128)(2,1)S(1)} %copy-done), kind=kOutput, calls=%fused_computation.10 | convolution fusion | flops 536870912 | bytes 5505024 | tf_op jit(solution)/shard_map/dot_general | solution.py:60
  183.5 4.5 %fusion.8 = f32[2048,128]{1,0:T(8,128)} fusion(bf16[2048,1024]{1,0:T(8,128)(2,1)} %constant_dynamic-update-slice_fusion, bf16[9,1024,128]{2,1,0:T(8,128)(2,1)S(1)} %copy-done), kind=kOutput, calls=%fused_computation.8 | convolution fusion | flops 536870912 | bytes 5505024 | tf_op jit(solution)/shard_map/dot_general | solution.py:60
  188.0 4.4 %fusion.6 = f32[2048,128]{1,0:T(8,128)} fusion(bf16[2048,1024]{1,0:T(8,128)(2,1)} %constant_dynamic-update-slice_fusion, bf16[9,1024,128]{2,1,0:T(8,128)(2,1)S(1)} %copy-done), kind=kOutput, calls=%fused_computation.6 | convolution fusion | flops 536870912 | bytes 5505024 | tf_op jit(solution)/shard_map/dot_general | solution.py:60
  192.4 4.4 %fusion.4 = f32[2048,128]{1,0:T(8,128)} fusion(bf16[2048,1024]{1,0:T(8,128)(2,1)} %constant_dynamic-update-slice_fusion, bf16[9,1024,128]{2,1,0:T(8,128)(2,1)S(1)} %copy-done), kind=kOutput, calls=%fused_computation.4 | convolution fusion | flops 536870912 | bytes 5505024 | tf_op jit(solution)/shard_map/dot_general | solution.py:60
  196.9 4.4 %fusion.2 = f32[2048,128]{1,0:T(8,128)} fusion(bf16[2048,1024]{1,0:T(8,128)(2,1)} %constant_dynamic-update-slice_fusion, bf16[9,1024,128]{2,1,0:T(8,128)(2,1)S(1)} %copy-done), kind=kOutput, calls=%fused_computation.2 | convolution fusion | flops 536870912 | bytes 5505024 | tf_op jit(solution)/shard_map/dot_general | solution.py:60
  201.3 4.5 %fusion = f32[2048,128]{1,0:T(8,128)} fusion(bf16[2048,1024]{1,0:T(8,128)(2,1)} %constant_dynamic-update-slice_fusion, bf16[9,1024,128]{2,1,0:T(8,128)(2,1)S(1)} %copy-done), kind=kOutput, calls=%fused_computation | convolution fusion | flops 536870912 | bytes 5505024 | tf_op jit(solution)/shard_map/dot_general | solution.py:60
  205.8 3.4 %fusion.66 = f32[2048,128]{1,0:T(8,128)S(1)} fusion(bf16[2048,1024]{1,0:T(8,128)(2,1)} %constant_dynamic-update-slice_fusion, bf16[9,1024,128]{2,1,0:T(8,128)(2,1)S(1)} %copy-done), kind=kOutput, calls=%fused_computation.48 | convolution fusion | flops 536870912 | bytes 5505024 | tf_op jit(solution)/shard_map/dot_general | solution.py:60
  209.2 8.6 %convolution_convert_fusion = bf16[2048,1024]{1,0:T(8,128)(2,1)} fusion(bf16[128,1024]{0,1:T(8,128)(2,1)S(1)} %all_gather.11, f32[2048,128]{1,0:T(8,128)} %fusion, f32[2048,128]{1,0:T(8,128)} %fusion.2, f32[2048,128]{1,0:T(8,128)} %fusion.4, f32[2048,128]{1,0:T(8,128)} %fusion.6, f32[2048,128]{1,0:T(8,128)S(1)} %fusion.66, f32[2048,128]{1,0:T(8,128)} %fusion.8, ...), kind=kOutput, calls=%fused_computation.16 | convolution fusion | flops 1078460416 | bytes 17301504 | tf_op jit(solution)/shard_map/dot_general | solution.py:68
  217.9 75.6 %reduce-scatter.2.cloned.1.call-done = bf16[128,1024]{1,0:T(8,128)(2,1)} async-done(((bf16[2048,1024]{1,0:T(8,128)(2,1)}), bf16[128,1024]{1,0:T(8,128)(2,1)}) %reduce-scatter.2.cloned.1.call-update) | async-done | bytes 262160 | tf_op jit(solution)/shard_map/reduce_scatter | solution.py:67
  293.5 1.1 fusion.60
  294.6 1.2 multiply_reduce_fusion
  295.8 1.8 fusion.61
  (36 shorter events, 7.0 us)
Async XLA Ops:
  6.5 94.2 %copy-start.1 = (bf16[128,32]{0,1:T(8,128)(2,1)S(1)}, bf16[128,32]{0,1:T(8,128)(2,1)}, u32[]{:S(2)}) copy-start(bf16[128,32]{0,1:T(8,128)(2,1)} %param.8) | copy-start | bytes 24580
  6.5 287.0 %reduce-scatter.2.cloned.1.call-start = ((), (), s32[]{:S(2)}) async-start(), calls=%async_computation.1 | async-start | bytes 4456448 | tf_op jit(solution)/shard_map/reduce_scatter | solution.py:67
  70.4 9.5 %collective-permute-start = (bf16[128,1024]{1,0:T(8,128)(2,1)S(1)}, bf16[128,1024]{1,0:T(8,128)(2,1)S(1)}, u32[]{:S(2)}, u32[]{:S(2)}) collective-permute-start(bf16[128,1024]{1,0:T(8,128)(2,1)S(1)} %get-tuple-element.6), channel_id=1, source_target_pairs={{0,1},{1,2},{2,3},{3,4},{4,5},{5,6},{6,7},{7,8},{8,9},{9,10},{10,1... | collective-permute-start | bytes 786440 | tf_op jit(solution)/shard_map/ppermute | solution.py:27
  73.4 8.4 %collective-permute-start.1 = (bf16[128,1024]{1,0:T(8,128)(2,1)S(1)}, bf16[128,1024]{1,0:T(8,128)(2,1)S(1)}, u32[]{:S(2)}, u32[]{:S(2)}) collective-permute-start(bf16[128,1024]{1,0:T(8,128)(2,1)S(1)} %get-tuple-element.6), channel_id=1, source_target_pairs={{0,15},{1,0},{2,1},{3,2},{4,3},{5,4},{6,5},{7,6},{8,7},{9,8},{10,9... | collective-permute-start | bytes 786440 | tf_op jit(solution)/shard_map/ppermute | solution.py:32
  79.9 9.5 %collective-permute-start.2 = (bf16[128,1024]{1,0:T(8,128)(2,1)S(1)}, bf16[128,1024]{1,0:T(8,128)(2,1)S(1)}, u32[]{:S(2)}, u32[]{:S(2)}) collective-permute-start(bf16[128,1024]{1,0:T(8,128)(2,1)S(1)} %collective-permute-done), channel_id=1, source_target_pairs={{0,1},{1,2},{2,3},{3,4},{4,5},{5,6},{6,7},{7,8},{8,9},{9,10},{10,1... | collective-permute-start | bytes 786440 | tf_op jit(solution)/shard_map/ppermute | solution.py:27
  81.8 9.5 %collective-permute-start.3 = (bf16[128,1024]{1,0:T(8,128)(2,1)S(1)}, bf16[128,1024]{1,0:T(8,128)(2,1)S(1)}, u32[]{:S(2)}, u32[]{:S(2)}) collective-permute-start(bf16[128,1024]{1,0:T(8,128)(2,1)S(1)} %collective-permute-done.1), channel_id=1, source_target_pairs={{0,15},{1,0},{2,1},{3,2},{4,3},{5,4},{6,5},{7,6},{8,7},{9,8},{10,9... | collective-permute-start | bytes 786440 | tf_op jit(solution)/shard_map/ppermute | solution.py:32
  89.4 9.5 %collective-permute-start.4 = (bf16[128,1024]{1,0:T(8,128)(2,1)S(1)}, bf16[128,1024]{1,0:T(8,128)(2,1)S(1)}, u32[]{:S(2)}, u32[]{:S(2)}) collective-permute-start(bf16[128,1024]{1,0:T(8,128)(2,1)S(1)} %collective-permute-done.2), channel_id=1, source_target_pairs={{0,1},{1,2},{2,3},{3,4},{4,5},{5,6},{6,7},{7,8},{8,9},{9,10},{10,1... | collective-permute-start | bytes 786440 | tf_op jit(solution)/shard_map/ppermute | solution.py:27
  91.3 35.0 %collective-permute-start.5 = (bf16[128,1024]{1,0:T(8,128)(2,1)S(1)}, bf16[128,1024]{1,0:T(8,128)(2,1)S(1)}, u32[]{:S(2)}, u32[]{:S(2)}) collective-permute-start(bf16[128,1024]{1,0:T(8,128)(2,1)S(1)} %collective-permute-done.3), channel_id=1, source_target_pairs={{0,15},{1,0},{2,1},{3,2},{4,3},{5,4},{6,5},{7,6},{8,7},{9,8},{10,9... | collective-permute-start | bytes 786440 | tf_op jit(solution)/shard_map/ppermute | solution.py:32
  98.8 33.4 %collective-permute-start.6 = (bf16[128,1024]{1,0:T(8,128)(2,1)S(1)}, bf16[128,1024]{1,0:T(8,128)(2,1)S(1)}, u32[]{:S(2)}, u32[]{:S(2)}) collective-permute-start(bf16[128,1024]{1,0:T(8,128)(2,1)S(1)} %collective-permute-done.4), channel_id=1, source_target_pairs={{0,1},{1,2},{2,3},{3,4},{4,5},{5,6},{6,7},{7,8},{8,9},{9,10},{10,1... | collective-permute-start | bytes 786440 | tf_op jit(solution)/shard_map/ppermute | solution.py:27
  125.5 50.1 %copy-start = (bf16[9,1024,128]{2,1,0:T(8,128)(2,1)S(1)}, bf16[9,1024,128]{2,1,0:T(8,128)(2,1)}, u32[]{:S(2)}) copy-start(bf16[9,1024,128]{2,1,0:T(8,128)(2,1)} %param.7) | copy-start | bytes 7077892
  126.2 11.5 %collective-permute-start.7 = (bf16[128,1024]{1,0:T(8,128)(2,1)S(1)}, bf16[128,1024]{1,0:T(8,128)(2,1)S(1)}, u32[]{:S(2)}, u32[]{:S(2)}) collective-permute-start(bf16[128,1024]{1,0:T(8,128)(2,1)S(1)} %collective-permute-done.5), channel_id=1, source_target_pairs={{0,15},{1,0},{2,1},{3,2},{4,3},{5,4},{6,5},{7,6},{8,7},{9,8},{10,9... | collective-permute-start | bytes 786440 | tf_op jit(solution)/shard_map/ppermute | solution.py:32
  132.2 11.8 %collective-permute-start.8 = (bf16[128,1024]{1,0:T(8,128)(2,1)S(1)}, bf16[128,1024]{1,0:T(8,128)(2,1)S(1)}, u32[]{:S(2)}, u32[]{:S(2)}) collective-permute-start(bf16[128,1024]{1,0:T(8,128)(2,1)S(1)} %collective-permute-done.6), channel_id=1, source_target_pairs={{0,1},{1,2},{2,3},{3,4},{4,5},{5,6},{6,7},{7,8},{8,9},{9,10},{10,1... | collective-permute-start | bytes 786440 | tf_op jit(solution)/shard_map/ppermute | solution.py:27
  137.7 11.1 %collective-permute-start.9 = (bf16[128,1024]{1,0:T(8,128)(2,1)S(1)}, bf16[128,1024]{1,0:T(8,128)(2,1)S(1)}, u32[]{:S(2)}, u32[]{:S(2)}) collective-permute-start(bf16[128,1024]{1,0:T(8,128)(2,1)S(1)} %collective-permute-done.7), channel_id=1, source_target_pairs={{0,15},{1,0},{2,1},{3,2},{4,3},{5,4},{6,5},{7,6},{8,7},{9,8},{10,9... | collective-permute-start | bytes 786440 | tf_op jit(solution)/shard_map/ppermute | solution.py:32
  144.1 11.1 %collective-permute-start.10 = (bf16[128,1024]{1,0:T(8,128)(2,1)S(1)}, bf16[128,1024]{1,0:T(8,128)(2,1)S(1)}, u32[]{:S(2)}, u32[]{:S(2)}) collective-permute-start(bf16[128,1024]{1,0:T(8,128)(2,1)S(1)} %collective-permute-done.8), channel_id=1, source_target_pairs={{0,1},{1,2},{2,3},{3,4},{4,5},{5,6},{6,7},{7,8},{8,9},{9,10},{10,1... | collective-permute-start | bytes 786440 | tf_op jit(solution)/shard_map/ppermute | solution.py:27
  148.8 10.2 %collective-permute-start.11 = (bf16[128,1024]{1,0:T(8,128)(2,1)S(1)}, bf16[128,1024]{1,0:T(8,128)(2,1)S(1)}, u32[]{:S(2)}, u32[]{:S(2)}) collective-permute-start(bf16[128,1024]{1,0:T(8,128)(2,1)S(1)} %collective-permute-done.9), channel_id=1, source_target_pairs={{0,15},{1,0},{2,1},{3,2},{4,3},{5,4},{6,5},{7,6},{8,7},{9,8},{10,9... | collective-permute-start | bytes 786440 | tf_op jit(solution)/shard_map/ppermute | solution.py:32
  155.1 10.2 %collective-permute-start.12 = (bf16[128,1024]{1,0:T(8,128)(2,1)S(1)}, bf16[128,1024]{1,0:T(8,128)(2,1)S(1)}, u32[]{:S(2)}, u32[]{:S(2)}) collective-permute-start(bf16[128,1024]{1,0:T(8,128)(2,1)S(1)} %collective-permute-done.10), channel_id=1, source_target_pairs={{0,1},{1,2},{2,3},{3,4},{4,5},{5,6},{6,7},{7,8},{8,9},{9,10},{10,1... | collective-permute-start | bytes 786440 | tf_op jit(solution)/shard_map/ppermute | solution.py:27
  159.0 9.9 %collective-permute-start.13 = (bf16[128,1024]{1,0:T(8,128)(2,1)S(1)}, bf16[128,1024]{1,0:T(8,128)(2,1)S(1)}, u32[]{:S(2)}, u32[]{:S(2)}) collective-permute-start(bf16[128,1024]{1,0:T(8,128)(2,1)S(1)} %collective-permute-done.11), channel_id=1, source_target_pairs={{0,15},{1,0},{2,1},{3,2},{4,3},{5,4},{6,5},{7,6},{8,7},{9,8},{10,9... | collective-permute-start | bytes 786440 | tf_op jit(solution)/shard_map/ppermute | solution.py:32
  165.4 9.5 %collective-permute-start.14 = (bf16[128,1024]{1,0:T(8,128)(2,1)S(1)}, bf16[128,1024]{1,0:T(8,128)(2,1)S(1)}, u32[]{:S(2)}, u32[]{:S(2)}) collective-permute-start(bf16[128,1024]{1,0:T(8,128)(2,1)S(1)} %collective-permute-done.12), channel_id=1, source_target_pairs={{0,1},{1,2},{2,3},{3,4},{4,5},{5,6},{6,7},{7,8},{8,9},{9,10},{10,1... | collective-permute-start | bytes 786440 | tf_op jit(solution)/shard_map/ppermute | solution.py:27
  217.9 77.9 %copy-start.2 = (f32[1024]{0:T(1024)S(1)}, f32[1024]{0:T(1024)}, u32[]{:S(2)}) copy-start(f32[1024]{0:T(1024)} %param.9) | copy-start | bytes 12292
Sparse Core Ops, SparseCore 0:
  218.0 75.4 reduce-scatter.1
